TPU v7x, 128 devices: a whole 4x4x4 slice. The times are simulated.
128 devices in a mesh: dp: 8 (over y, core), fsdp: 16 (over z, x).
Axes of the slice: x: 4, y: 4, z: 4, core: 2. Of those that a mesh axis runs over, the one named last changes fastest.
Arguments:
- attn_out: bfloat16 [32768, 3072], P(('dp', 'fsdp')), may hold values from -0.078125 to 0.078125
- out_grad: bfloat16 [32768, 3072], P(('dp', 'fsdp')), may hold values from -24 to 24
- weight: bfloat16 [3072, 3072], P('fsdp'), may hold values from -0.109375 to 0.109375
- sign_vector: int32 [3072], replicated, may hold values from -1 to 1, as said below
Outputs:
- input_grad: bfloat16 [32768, 3072], P(('dp', 'fsdp'))
- weight_grad: float32 [3072, 3072], P('fsdp', 'dp')
Inputs may be any that keep to these rules, and one draw needn't show every extreme that they name: `sign_vector`: each entry is -1 or +1.
All inputs are finite; a program needn't handle non-finite values.
Results may differ from a plain program's by a relative error of at most 0.004.
Values may be sent and summed in bfloat16 or wider, within the bound.
A program may use at most 128 MiB of HBM per device.

v0:
```python
import math

import jax
import jax.numpy as jnp
from jax import lax
from jax.sharding import PartitionSpec as P

BLOCK = 128


EPSILON = 1e-06


def hadamard():
    position = jnp.arange(BLOCK, dtype=jnp.int32)
    common = jnp.bitwise_and(position[:, None], position[None, :])
    parity = jnp.zeros((BLOCK, BLOCK), jnp.int32)
    for shift_bits in range(BLOCK.bit_length() - 1):
        parity = parity + jnp.bitwise_and(jnp.right_shift(common, shift_bits), 1)
    signed = 1 - 2 * jnp.bitwise_and(parity, 1)
    return signed.astype(jnp.float32) / math.sqrt(BLOCK)


def rotate(matrix, rotation):
    row_count, col_count = matrix.shape
    blocks = matrix.reshape(row_count, col_count // BLOCK, BLOCK)
    return jnp.einsum("rbk,kj->rbj", blocks, rotation, precision=lax.Precision.HIGHEST)


def body(attn_out, out_grad, weight, sign_vector):
    rotation = hadamard()
    sign_row = sign_vector.astype(jnp.float32)
    row_count = weight.shape[0]
    gathered = lax.all_gather(out_grad, "fsdp", axis=0, tiled=True)
    columns = lax.all_to_all(attn_out, "fsdp", split_axis=1, concat_axis=0, tiled=True)
    input_grad = lax.dot_general(
        out_grad,
        lax.all_gather(weight, "fsdp", axis=0, tiled=True),
        (((1,), (1,)), ((), ())),
        preferred_element_type=jnp.float32,
    ).astype(jnp.bfloat16)
    partial_value = lax.dot_general(
        columns, gathered, (((0,), (0,)), ((), ())), preferred_element_type=jnp.float32
    )
    turned = rotate(partial_value * sign_row[None, :], rotation)
    scale = lax.pmax(jnp.max(jnp.abs(turned), axis=2), "dp") + EPSILON
    quant = jnp.floor(turned * 127.0 / scale[:, :, None] + 0.5).reshape(row_count, -1)
    summed = lax.psum_scatter(
        quant.astype(jnp.bfloat16), "dp", scatter_dimension=1, tiled=True
    ).astype(jnp.float32)
    share_width = summed.shape[1]
    share_blocks = share_width // BLOCK
    dp_index = lax.axis_index("dp")
    my_scale = lax.dynamic_slice_in_dim(scale, dp_index * share_blocks, share_blocks, 1)
    my_signs = lax.dynamic_slice_in_dim(sign_row, dp_index * share_width, share_width, 0)
    restored = (
        summed.reshape(row_count, share_blocks, BLOCK) * (my_scale[:, :, None] / 127.0)
    ).reshape(row_count, share_width)
    weight_grad = rotate(restored, rotation).reshape(row_count, share_width) * my_signs[None, :]
    return (input_grad, weight_grad)


def solution(mesh):
    in_specs = (P(("dp", "fsdp"), None), P(("dp", "fsdp"), None), P("fsdp", None), P())
    out_specs = (P(("dp", "fsdp"), None), P("fsdp", "dp"))
    return jax.shard_map(body, mesh=mesh, in_specs=in_specs, out_specs=out_specs, check_vma=False)
```

profile of v0, /device:TPU:4, one launch (start us, length us, event | category | flops | bytes accessed | tf_op | source)
XLA Modules:
  0.0 345.0 jit_solution(11800710766111427035)
XLA Ops:
  7.2 0.7 all-gather.5.cloned.1.call-update
  8.0 0.7 all-gather.3.cloned.1.call-update
  8.7 1.6 copy.11
  10.2 8.4 %all-to-all-start = ((bf16[256,16,192]{0,2,1:T(8,128)(2,1)}), bf16[256,16,192]{0,2,1:T(8,128)(2,1)S(1)}, u32[]{:S(2)}, u32[]{:S(2)}) async-start(bf16[256,16,192]{0,2,1:T(8,128)(2,1)} %bitcast), calls=%async_computation | async-start | bytes 3145728 | tf_op jit(solution)/shard_map/all_to_all | solution.py:35
  18.7 0.1 dynamic_slice.7
  18.8 29.6 %all-to-all-done = bf16[256,16,192]{0,2,1:T(8,128)(2,1)S(1)} async-done(((bf16[256,16,192]{0,2,1:T(8,128)(2,1)}), bf16[256,16,192]{0,2,1:T(8,128)(2,1)S(1)}, u32[]{:S(2)}, u32[]{:S(2)}) %all-to-all-start) | async-done | bytes 1572896 | tf_op jit(solution)/shard_map/all_to_all | solution.py:35
  48.4 0.2 copy.18
  48.6 128.5 %all-gather.5.cloned.1.call-done = bf16[4096,3072]{1,0:T(8,128)(2,1)} async-done(((bf16[256,3072]{1,0:T(8,128)(2,1)}), bf16[4096,3072]{1,0:T(8,128)(2,1)}) %all-gather.5.cloned.1.call-update) | async-done | bytes 25165840 | tf_op jit(solution)/shard_map/all_gather | solution.py:34
  177.1 10.8 %fusion = f32[24,8,24,128]{3,1,2,0:T(8,128)S(1)} fusion(bf16[4096,192]{0,1:T(8,128)(2,1)S(1)} %bitcast.30, bf16[4096,3072]{1,0:T(8,128)(2,1)} %all-gather.5.cloned.1.call-done, f32[3072]{0:T(1024)S(1)} %convert_element_type.19), kind=kOutput, calls=%fused_computation.4 | convolution fusion | flops 4832428032 | bytes 29110272 | tf_op jit(solution)/shard_map/dot_general | solution.py:42
  187.9 0.4 copy.20
  188.3 2.2 abs_reduce_fusion
  190.5 27.7 %pmax.7 = f32[192,24]{1,0:T(8,128)S(1)} all-reduce(f32[192,24]{1,0:T(8,128)S(1)} %get-tuple-element.2), channel_id=1, replica_groups=mesh['dp'=8,'fsdp'=16] {'dp'}, use_global_device_ids=true, to_apply=%region_1.0 | all-reduce | flops 4608 | bytes 36864 | tf_op jit(solution)/shard_map/pmax | solution.py:46
  218.2 0.6 copy-done.2
  218.8 0.8 floor_convert_fusion
  219.6 2.0 copy.17
  221.7 79.3 %all-gather.3.cloned.1.call-done = bf16[3072,3072]{1,0:T(8,128)(2,1)} async-done(((bf16[192,3072]{1,0:T(8,128)(2,1)}), bf16[3072,3072]{1,0:T(8,128)(2,1)}) %all-gather.3.cloned.1.call-update) | async-done | bytes 18874384 | tf_op jit(solution)/shard_map/all_gather | solution.py:38
  301.0 10.4 %convolution_convert_fusion = bf16[256,3072]{1,0:T(8,128)(2,1)} fusion(bf16[256,3072]{1,0:T(8,128)(2,1)S(1)} %copy-done.1, bf16[3072,3072]{1,0:T(8,128)(2,1)} %all-gather.3.cloned.1.call-done), kind=kOutput, calls=%fused_computation.1 | convolution fusion | flops 4832624640 | bytes 22020096 | tf_op jit(solution)/shard_map/dot_general | solution.py:36
  311.4 0.1 dynamic-slice_multiply_fusion
  311.5 24.4 %reduce-scatter.4.cloned.1.call-done = bf16[384,192]{1,0:T(8,128)(2,1)} async-done(((bf16[3072,192]{1,0:T(8,128)(2,1)}), bf16[384,192]{1,0:T(8,128)(2,1)}) %reduce-scatter.4.cloned.1.call-update) | async-done | bytes 147472
  335.8 1.1 copy.16
  336.9 0.1 reshape.31
  337.0 0.3 broadcast_multiply_fusion
  337.3 0.4 convolution_bitcast_fusion
  337.7 0.7 bitcast_multiply_fusion
  (15 shorter events, 0.2 us)
Async XLA Ops:
  7.2 1.5 copy-start
  7.2 169.9 %all-gather.5.cloned.1.call-start = ((), (), s32[]{:S(2)}) async-start(), calls=%async_computation.3 | async-start | bytes 26738688 | tf_op jit(solution)/shard_map/all_gather | solution.py:34
  7.9 293.1 %all-gather.3.cloned.1.call-start = ((), (), s32[]{:S(2)}) async-start(), calls=%async_computation.2 | async-start | bytes 20054016 | tf_op jit(solution)/shard_map/all_gather | solution.py:38
  10.2 8.5 %copy-start.4 = (s32[3072]{0:T(1024)S(1)}, s32[3072]{0:T(1024)}, u32[]{:S(2)}) copy-start(s32[3072]{0:T(1024)} %param.7) | copy-start | bytes 36868
  10.2 38.1 %all-to-all-start = ((bf16[256,16,192]{0,2,1:T(8,128)(2,1)}), bf16[256,16,192]{0,2,1:T(8,128)(2,1)S(1)}, u32[]{:S(2)}, u32[]{:S(2)}) async-start(bf16[256,16,192]{0,2,1:T(8,128)(2,1)} %bitcast), calls=%async_computation | async-start | bytes 3145728 | tf_op jit(solution)/shard_map/all_to_all | solution.py:35
  18.7 317.2 %reduce-scatter.4.cloned.1.call-start = ((), (), s32[]{:S(2)}) async-start(), calls=%async_computation.4 | async-start | bytes 1769472
  218.2 0.6 copy-start.2
  219.6 81.4 %copy-start.1 = (bf16[256,3072]{1,0:T(8,128)(2,1)S(1)}, bf16[256,3072]{1,0:T(8,128)(2,1)}, u32[]{:S(2)}) copy-start(bf16[256,3072]{1,0:T(8,128)(2,1)} %param.5) | copy-start | bytes 4718596
  221.7 89.7 %copy-start.3 = (f32[192,24]{1,0:T(8,128)S(1)}, f32[192,24]{1,0:T(8,128)}, u32[]{:S(2)}) copy-start(f32[192,24]{1,0:T(8,128)} %copy-done.2) | copy-start | bytes 55300
Sparse Core Ops, SparseCore 0:
  10.2 166.8 all-gather.4
  179.2 121.7 all-gather.2
  303.4 32.3 reduce-scatter.3
where the time goes:
time: 345 us
  waiting for transfers between devices  263 us (76%)
  blocking collectives  27.7 us (8%)
  matrix products  23.8 us (7%)
  between operations  13.9 us (4%)
  starting transfers between devices  8.54 us (2%)
  local copies, waits for them, and re-layouts  6.09 us (2%)
    all_gather x1, waiting for transfers between devices, body(): gathered = lax.all_gather(out_grad, 'fsdp', axis=0, tiled=True)  129 us
    all_gather x1, waiting for transfers between devices, body(): lax.all_gather(weight, 'fsdp', axis=0, tiled=True)  79.3 us
    all_to_all x1, waiting for transfers between devices, body(): lax.all_to_all(attn_out, 'fsdp', split_axis=1, concat_axis=0, tiled=True)  29.6 us
    pmax x1, blocking collectives, body(): scale = lax.pmax(jnp.max(jnp.abs(turned), axis=2), 'dp') + EPSILON  27.7 us
    unnamed x4, waiting for transfers between devices  25.7 us
    dot_general x1, matrix products, body(): lax.dot_general(columns, gathered, (((0,), (0,)), ((), ())), preferred_el...  10.8 us
    dot_general x1, matrix products, body(): lax.dot_general(out_grad, lax.all_gather(weight, 'fsdp', axis=0, tiled=Tr...  10.4 us
    all_to_all x1, starting transfers between devices, body(): lax.all_to_all(attn_out, 'fsdp', split_axis=1, concat_axis=0, tiled=True)  8.42 us
  transfers between devices with their start and end apart: 4, of which 4 were waited for; matrix products, arithmetic and copies ran while one was open for 8% of the time, Pallas kernels for 0%

commit v1 on v0

v1 whole, which is shorter than its diff:
```python
import functools
import math

import jax
import jax.numpy as jnp
from jax import lax
from jax.experimental import pallas as pl
from jax.experimental.pallas import tpu as pltpu
from jax.sharding import PartitionSpec as P

BLOCK = 128
EPSILON = 1e-06
SIDE = 4
TOK = 256
SHARD = 192
TILE = 768
HALF = 384
FEATURES = 3072
MESH = pl.DeviceIdType.MESH


def hadamard_signs():
    row = lax.broadcasted_iota(jnp.int32, (BLOCK, BLOCK), 0)
    col = lax.broadcasted_iota(jnp.int32, (BLOCK, BLOCK), 1)
    common = jnp.bitwise_and(row, col)
    parity = jnp.zeros((BLOCK, BLOCK), jnp.int32)
    for shift in range(BLOCK.bit_length() - 1):
        parity = parity + jnp.bitwise_and(jnp.right_shift(common, shift), 1)
    signed = 1 - 2 * jnp.bitwise_and(parity, 1)
    return signed.astype(jnp.float32).astype(jnp.bfloat16)


def rotate(value, had):
    high = value.astype(jnp.bfloat16)
    rest = value - high.astype(jnp.float32)
    middle = rest.astype(jnp.bfloat16)
    low = (rest - middle.astype(jnp.float32)).astype(jnp.bfloat16)
    total = jnp.dot(low, had, preferred_element_type=jnp.float32)
    total = total + jnp.dot(middle, had, preferred_element_type=jnp.float32)
    total = total + jnp.dot(high, had, preferred_element_type=jnp.float32)
    return total * (1.0 / math.sqrt(BLOCK))


def kernel(
    a_ref, g_ref, w_ref, sign_ref, ig_ref, wg_ref,
    attn, grad, wbuf, g_own, ig_acc, acc, had_ref, maxima, quant, sib_in, summed, pieces, peaks, scale, scale_t,
    local_sem, a_s, a_r, g_s, g_r, w_s, w_r, h_s, h_r, m_s, m_r, q_s, q_r, p_s, p_r, c_s, c_r,
):
    dp, fsdp = lax.axis_index("dp"), lax.axis_index("fsdp")
    y, c = dp // 2, lax.rem(dp, 2)
    z, x = fsdp // SIDE, lax.rem(fsdp, SIDE)
    s = 1 - 2 * c
    off = [0, -s, s, 2]

    def mod(v):
        return lax.rem(v + 2 * SIDE, SIDE)

    def device(dx=0, dy=0, dz=0, dc=0):
        return (2 * mod(y + dy) + lax.rem(c + dc, 2), SIDE * mod(z + dz) + mod(x + dx))

    def remote(src, dst, send, recv, target):
        copy = pltpu.make_async_remote_copy(
            src_ref=src, dst_ref=dst, send_sem=send, recv_sem=recv, device_id=target, device_id_type=MESH
        )
        return copy

    sent = []

    def push(*args):
        copy = remote(*args)
        copy.start()
        sent.append(copy)
        return copy

    barrier = pltpu.get_barrier_semaphore()
    greeted = [device(dx=d) for d in range(1, SIDE)] + [device(dz=d) for d in range(1, SIDE)]
    greeted += [(lax.rem(dp + d, 8), fsdp) for d in range(1, 8)]
    for target in greeted:
        pl.semaphore_signal(barrier, inc=1, device_id=target, device_id_type=MESH)
    diagonal = x == y
    for k in range(SIDE):

        @pl.when(jnp.logical_not(jnp.logical_and(diagonal, k == y)))
        def _():
            pl.semaphore_signal(barrier, inc=1, device_id=(2 * k + c, SIDE * z + y), device_id_type=MESH)

    pl.semaphore_wait(barrier, len(greeted) + SIDE - diagonal.astype(jnp.int32))

    def shard_of(pa, pb):
        on_z = lax.select(c == 1, mod(z + off[pa]), mod(z + off[pb]))
        on_x = lax.select(c == 1, mod(x + off[pb]), mod(x + off[pa]))
        return SIDE * on_z + on_x

    def part_of(py, core=c):
        return 2 * mod(y + off[py]) + core

    def w_chunk(pa, pb, py):
        return wbuf.at[
            pl.ds(pl.multiple_of(SHARD * shard_of(pa, pb), SHARD), SHARD),
            pl.ds(pl.multiple_of(HALF * part_of(py), HALF), HALF),
        ]

    def along_a(d):
        return device(dx=lax.select(c == 1, 0, d), dz=lax.select(c == 1, d, 0))

    def along_b(d):
        return device(dx=lax.select(c == 1, d, 0), dz=lax.select(c == 1, 0, d))

    w_copies = {}

    def w_push(src, pa, pb, py, landing, target):
        ta, tb, ty = landing
        index = 16 * ty + 4 * tb + ta
        w_copies[landing] = push(src, w_chunk(pa, pb, py), w_s.at[index], w_r.at[index], target)

    w_own = w_ref.at[:, pl.ds(pl.multiple_of(HALF * dp, HALF), HALF)]
    w_push(w_own, 0, 0, 0, (1, 0, 0), along_a(s))
    w_push(w_own, 0, 0, 0, (2, 0, 0), along_a(-s))
    w_push(w_own, 0, 0, 0, (0, 1, 0), along_b(s))
    w_push(w_own, 0, 0, 0, (0, 2, 0), along_b(-s))

    def a_block(jx, kz):
        return attn.at[jx, pl.ds(TOK * kz, TOK)]

    def g_block(jx, kz):
        return grad.at[jx, pl.ds(TOK * kz, TOK)]

    def a_columns(owner):
        return a_ref.at[:, pl.ds(pl.multiple_of(TILE * owner, TILE), TILE)]

    def g_columns(owner):
        return g_ref.at[:, pl.ds(pl.multiple_of(TILE * owner, TILE), TILE)]

    a_copies, g_copies = {}, {}

    def a_push(src, landing, target):
        index = 4 * landing[0] + landing[1]
        a_copies[landing] = push(src, a_block(*landing), a_s.at[index], a_r.at[index], target)

    def g_push(src, landing, target):
        index = 4 * landing[0] + landing[1]
        g_copies[landing] = push(src, g_block(*landing), g_s.at[index], g_r.at[index], target)

    local = [
        pltpu.make_async_copy(a_columns(z), a_block(0, 0), local_sem.at[0]),
        pltpu.make_async_copy(g_columns(x), g_block(0, 0), local_sem.at[1]),
        pltpu.make_async_copy(g_ref, g_own, local_sem.at[2]),
    ]
    for py in range(SIDE):
        columns = pl.ds(pl.multiple_of(HALF * part_of(py), HALF), HALF)
        local.append(pltpu.make_async_copy(w_ref.at[:, columns], w_chunk(0, 0, py), local_sem.at[3 + py]))
    for copy in local:
        copy.start()
    for position, d in ((1, s), (2, -s), (3, 2)):
        a_push(a_columns(mod(z + d)), (0, position), device(dz=d))
        g_push(g_columns(mod(x + d)), (position, 0), device(dx=d))

    def a_spread(kz):
        a_push(a_block(0, kz), (1, kz), device(dx=s))
        a_push(a_block(0, kz), (2, kz), device(dx=-s))

    def g_spread(jx):
        g_push(g_block(jx, 0), (jx, 1), device(dz=s))
        g_push(g_block(jx, 0), (jx, 2), device(dz=-s))

    def w_spread_b(pa):
        w_push(w_chunk(pa, 0, 0), pa, 0, 0, (pa, 1, 0), along_b(s))
        w_push(w_chunk(pa, 0, 0), pa, 0, 0, (pa, 2, 0), along_b(-s))

    def w_spread_y(pa, pb):
        w_push(w_chunk(pa, pb, 0), pa, pb, 0, (pa, pb, 1), device(dy=s))
        w_push(w_chunk(pa, pb, 0), pa, pb, 0, (pa, pb, 2), device(dy=-s))

    def w_plane(pa, pb):
        w_copies[pa, pb, 0].wait_recv()
        if pb == 0:
            if pa == 1:
                w_push(w_chunk(1, 0, 0), 1, 0, 0, (3, 0, 0), along_a(s))
            w_spread_b(pa)
        if pb == 1:
            w_push(w_chunk(pa, 1, 0), pa, 1, 0, (pa, 3, 0), along_b(s))
        w_spread_y(pa, pb)

    def w_forward(pa, pb):
        w_copies[pa, pb, 1].wait_recv()
        w_push(w_chunk(pa, pb, 1), pa, pb, 1, (pa, pb, 3), device(dy=s))

    def share_copy(py, landing):
        columns = wbuf.at[:, pl.ds(pl.multiple_of(HALF * part_of(py), HALF), HALF)]
        return remote(columns, columns, h_s.at[py], h_r.at[landing], device(dc=1))

    def w_share(py):
        copy = share_copy(py, (0, 2, 1, 3)[py])
        copy.start()
        sent.append(copy)

    local[0].wait()
    a_spread(0)
    local[1].wait()
    g_spread(0)

    order = [
        (1, 0), (2, 0), (0, 1), (0, 2), (3, 0), (1, 1), (1, 2), (2, 1), (2, 2), (0, 3), (3, 1), (3, 2), (1, 3), (2, 3), (3, 3)
    ]
    for chunk in order[:4]:
        w_plane(*chunk)
    for position in (1, 2):
        a_copies[0, position].wait_recv()
        a_spread(position)
        g_copies[position, 0].wait_recv()
        g_spread(position)
    for chunk in order[4:9]:
        w_plane(*chunk)
    a_copies[0, 3].wait_recv()
    a_spread(3)
    g_copies[3, 0].wait_recv()
    g_spread(3)
    for chunk in order[:3]:
        w_forward(*chunk)
    for chunk in order[9:]:
        w_plane(*chunk)
    for copy in local[2:]:
        copy.wait()
    w_share(0)
    had_ref[...] = hadamard_signs()

    for i in range(SIDE):
        a_copies[1, i].wait_recv()
        a_push(a_block(1, i), (3, i), device(dx=s))
        g_copies[i, 1].wait_recv()
        g_push(g_block(i, 1), (i, 3), device(dz=s))
        for chunk in order[3 + 3 * i : 6 + 3 * i]:
            w_forward(*chunk)
    w_share(1)

    def partial_step(jx, low, high, first=False):
        def tile(m, carry):
            rows = pl.ds(pl.multiple_of(256 * m, 256), 256)
            value = lax.dot_general(
                attn[jx, TOK * low : TOK * high, rows],
                grad[jx, TOK * low : TOK * high, :],
                (((0,), (0,)), ((), ())),
                preferred_element_type=jnp.float32,
            )
            if first:
                acc[rows, :] = value
            else:
                acc[rows, :] += value
            return carry

        lax.fori_loop(0, TILE // 256, tile, 0)

    def input_step(py):
        share_copy(py, py).wait_recv()
        columns = pl.ds(pl.multiple_of(TILE * mod(y + off[py]), TILE), TILE)

        def tile(n, carry):
            rows = pl.ds(pl.multiple_of(512 * n, 512), 512)
            value = lax.dot_general(
                g_own[:, columns], wbuf[rows, columns], (((1,), (1,)), ((), ())), preferred_element_type=jnp.float32
            )
            if py == 0:
                ig_acc[:, rows] = value
            elif py < SIDE - 1:
                ig_acc[:, rows] += value
            else:
                ig_ref[:, rows] = (ig_acc[:, rows] + value).astype(ig_ref.dtype)
            return carry

        lax.fori_loop(0, FEATURES // 512, tile, 0)

    input_step(0)
    for i in range(SIDE):
        a_copies[2, i].wait_recv()
        g_copies[i, 2].wait_recv()
    for jx in range(3):
        partial_step(jx, 0, 3, first=jx == 0)
    for chunk in order:
        w_copies[chunk + (2,)].wait_recv()
    w_share(2)
    input_step(1)
    for i in range(SIDE):
        a_copies[3, i].wait_recv()
        g_copies[i, 3].wait_recv()
        if i < 3:
            partial_step(i, 3, 4)
    partial_step(3, 0, 4)

    maxima[...] = jnp.zeros_like(maxima)

    def turn(step, carry):
        b, m = step // 3, lax.rem(step, 3)
        rows = pl.ds(pl.multiple_of(256 * m, 256), 256)
        columns = pl.ds(pl.multiple_of(BLOCK * b, BLOCK), BLOCK)
        signs = sign_ref[:, pl.ds(pl.multiple_of(TILE * x + BLOCK * b, BLOCK), BLOCK)]
        turned = rotate(acc[rows, columns] * signs, had_ref[...])
        acc[rows, columns] = turned
        peak = jnp.max(jnp.abs(turned), axis=1, keepdims=True)
        lane = lax.broadcasted_iota(jnp.int32, (256, BLOCK), 1)
        maxima[rows, :] = jnp.where(lane == b, peak, maxima[rows, :])
        return carry

    lax.fori_loop(0, 18, turn, 0)
    for r in range(TILE // BLOCK):
        span = slice(BLOCK * r, BLOCK * r + BLOCK)
        peaks[0, :, span] = jnp.transpose(maxima[span, :])[:8]
    met = [
        push(peaks.at[0], peaks.at[d], m_s.at[d], m_r.at[d], (lax.rem(dp + d, 8), fsdp)) for d in range(1, 8)
    ]

    for chunk in order:
        w_copies[chunk + (3,)].wait_recv()
    w_share(3)

    for copy in met:
        copy.wait_recv()
    top = peaks[0]
    for d in range(1, 8):
        top = jnp.maximum(top, peaks[d])
    scale[0] = top + EPSILON
    for r in range(TILE // BLOCK):
        span = slice(BLOCK * r, BLOCK * r + BLOCK)
        scale_t[span, :] = jnp.transpose(
            jnp.concatenate([scale[0, :, span], jnp.ones((BLOCK - 8, BLOCK), jnp.float32)], axis=0)
        )

    for d in range(1, SIDE):

        @pl.when(diagonal)
        def _():
            remote(scale.at[0], scale.at[1], c_s.at[d], c_r.at[0], device(dx=d)).start()

    for b in range(TILE // BLOCK):
        columns = slice(BLOCK * b, BLOCK * b + BLOCK)

        def round_rows(m, carry):
            rows = pl.ds(pl.multiple_of(256 * m, 256), 256)
            factor = 127.0 / scale_t[rows, b : b + 1]
            quant[rows, columns] = jnp.floor(acc[rows, columns] * factor + 0.5).astype(quant.dtype)
            return carry

        lax.fori_loop(0, 3, round_rows, 0)

    mine = pl.ds(pl.multiple_of(HALF * c, HALF), HALF)
    other = pl.ds(pl.multiple_of(HALF * (1 - c), HALF), HALF)
    traded = push(quant.at[:, other], sib_in, q_s.at[0], q_r.at[0], device(dc=1))
    input_step(2)
    traded.wait_recv()
    summed[...] = quant[:, mine] + sib_in[...]

    def piece_copies(k):
        src = summed.at[pl.ds(SHARD * k, SHARD), :]
        here = pltpu.make_async_copy(src, pieces.at[y], p_s.at[k])
        away = remote(src, pieces.at[y], p_s.at[k], p_r.at[y], (2 * x + c, SIDE * z + k))
        return jnp.logical_and(diagonal, k == x), here, away

    for k in range(SIDE):
        stays, here, away = piece_copies(k)
        pl.when(stays)(here.start)
        pl.when(jnp.logical_not(stays))(away.start)

    input_step(3)

    for k in range(SIDE):
        stays, here, away = piece_copies(k)
        pl.when(stays)(here.wait)
        pl.when(jnp.logical_not(stays))(away.wait_send)
    for k in range(SIDE):
        arrives = remote(pieces.at[k], pieces.at[k], p_s.at[k], p_r.at[k], device(dx=1))
        pl.when(jnp.logical_not(jnp.logical_and(diagonal, k == y)))(arrives.wait_recv)

    @pl.when(jnp.logical_not(diagonal))
    def _():
        remote(scale.at[0], scale.at[1], c_s.at[0], c_r.at[0], device(dx=1)).wait_recv()

    @pl.when(diagonal)
    def _():
        scale[1] = scale[0]
        for d in range(1, SIDE):
            remote(scale.at[0], scale.at[1], c_s.at[d], c_r.at[0], device(dx=d)).wait_send()

    for r in range(TILE // BLOCK):
        span = slice(BLOCK * r, BLOCK * r + BLOCK)
        scale_t[span, :] = jnp.transpose(
            jnp.concatenate([scale[1, :, span], jnp.ones((BLOCK - 8, BLOCK), jnp.float32)], axis=0)
        )
    rows = pl.ds(pl.multiple_of(SHARD * x, SHARD), SHARD)
    factors = scale_t[rows, :] / 127.0
    for j in range(HALF // BLOCK):
        columns = slice(BLOCK * j, BLOCK * j + BLOCK)
        total = pieces[0, :, columns].astype(jnp.float32)
        for k in range(1, SIDE):
            total = total + pieces[k, :, columns].astype(jnp.float32)
        factor = jnp.where(c == 0, factors[:, j : j + 1], factors[:, 3 + j : 4 + j])
        signs = sign_ref[:, pl.ds(pl.multiple_of(HALF * dp + BLOCK * j, BLOCK), BLOCK)]
        wg_ref[:, columns] = rotate(total * factor, had_ref[...]) * signs

    for copy in sent:
        copy.wait_send()


def body(attn_out, out_grad, weight, sign_vector):
    signs = sign_vector.astype(jnp.float32)[None, :]
    hbm = pl.BlockSpec(memory_space=pl.ANY)
    vmem = pl.BlockSpec(memory_space=pltpu.VMEM)
    dma = pltpu.SemaphoreType.DMA
    return pl.pallas_call(
        kernel,
        out_shape=(
            jax.ShapeDtypeStruct((TOK, FEATURES), jnp.bfloat16),
            jax.ShapeDtypeStruct((SHARD, HALF), jnp.float32),
        ),
        in_specs=[hbm, hbm, hbm, vmem],
        out_specs=(vmem, vmem),
        scratch_shapes=[
            pltpu.VMEM((SIDE, SIDE * TOK, TILE), jnp.bfloat16),
            pltpu.VMEM((SIDE, SIDE * TOK, TILE), jnp.bfloat16),
            pltpu.VMEM((FEATURES, FEATURES), jnp.bfloat16),
            pltpu.VMEM((TOK, FEATURES), jnp.bfloat16),
            pltpu.VMEM((TOK, FEATURES), jnp.float32),
            pltpu.VMEM((TILE, TILE), jnp.float32),
            pltpu.VMEM((BLOCK, BLOCK), jnp.bfloat16),
            pltpu.VMEM((TILE, BLOCK), jnp.float32),
            pltpu.VMEM((TILE, TILE), jnp.bfloat16),
            pltpu.VMEM((TILE, HALF), jnp.bfloat16),
            pltpu.VMEM((TILE, HALF), jnp.bfloat16),
            pltpu.VMEM((SIDE, SHARD, HALF), jnp.bfloat16),
            pltpu.VMEM((8, 8, TILE), jnp.float32),
            pltpu.VMEM((2, 8, TILE), jnp.float32),
            pltpu.VMEM((TILE, BLOCK), jnp.float32),
            dma((8,)), dma((16,)), dma((16,)), dma((16,)), dma((16,)), dma((64,)), dma((64,)), dma((4,)), dma((4,)),
            dma((8,)), dma((8,)), dma((1,)), dma((1,)), dma((4,)), dma((4,)), dma((4,)), dma((1,)),
        ],
        compiler_params=pltpu.CompilerParams(
            collective_id=0, has_side_effects=True, vmem_limit_bytes=60 * 2**20
        ),
    )(attn_out, out_grad, weight, signs)


def solution(mesh):
    in_specs = (P(("dp", "fsdp"), None), P(("dp", "fsdp"), None), P("fsdp", None), P())
    out_specs = (P(("dp", "fsdp"), None), P("fsdp", "dp"))
    return jax.shard_map(body, mesh=mesh, in_specs=in_specs, out_specs=out_specs, check_vma=False)
```

time: 345 us -> 137 us (0.40)
  waiting for transfers between devices: 263 us -> 0 us
  Pallas kernels: 0 us -> 131 us
  blocking collectives: 27.7 us -> 0 us
  matrix products: 23.8 us -> 0 us
  between operations: 13.9 us -> 0.65 us
  starting transfers between devices: 8.54 us -> 0 us
    all_gather x2 -> x0, waiting for transfers between devices: 208 us -> none  [the longest x1 129 us: body(): gathered = lax.all_gather(out_grad, 'fsdp', axis=0, tiled=True)]
    pallas_call x0 -> x1, Pallas kernels: none -> 131 us  [body(): pl.pallas_call(kernel, out_shape=(jax.ShapeDtypeStruct((TOK, FEATURES), j...]
    all_to_all x1 -> x0, waiting for transfers between devices: 29.6 us -> none  [body(): lax.all_to_all(attn_out, 'fsdp', split_axis=1, concat_axis=0, tiled=True)]
    pmax x1 -> x0, blocking collectives: 27.7 us -> none  [body(): scale = lax.pmax(jnp.max(jnp.abs(turned), axis=2), 'dp') + EPSILON]
    unnamed x4 -> x0, waiting for transfers between devices: 25.7 us -> none
    dot_general x4 -> x0, matrix products: 23.8 us -> none  [the longest x1 10.8 us: body(): lax.dot_general(columns, gathered, (((0,), (0,)), ((), ())), preferred_el...]
    all_to_all x1 -> x0, starting transfers between devices: 8.42 us -> none  [body(): lax.all_to_all(attn_out, 'fsdp', split_axis=1, concat_axis=0, tiled=True)]
  transfers between devices with their start and end apart: 4 -> 0, of which waited for: 4 -> 0; matrix products, arithmetic and copies ran while one was open for 8% -> 0% of each run, Pallas kernels for 0% -> 0%
where the time goes in v1:
time: 137 us
  Pallas kernels  131 us (96%)
  local copies, waits for them, and re-layouts  3.41 us (2%)
    pallas_call x1, Pallas kernels, body(): pl.pallas_call(kernel, out_shape=(jax.ShapeDtypeStruct((TOK, FEATURES), j...  131 us
    unnamed x4, local copies, waits for them, and re-layouts  3.41 us

profile of v1, /device:TPU:4, one launch (start us, length us, event | category | flops | bytes accessed | tf_op | source)
XLA Modules:
  0.0 136.8 jit_solution(6061531868619269072)
XLA Ops:
  0.6 1.3 convert_element_type.3
  1.9 131.4 %shard_map.59 = (bf16[256,3072]{1,0:T(8,128)(2,1)}, f32[192,384]{1,0:T(8,128)}) custom-call(bf16[256,3072]{1,0:T(8,128)(2,1)} %a_ref.1, bf16[256,3072]{1,0:T(8,128)(2,1)} %g_ref.1, bf16[192,3072]{1,0:T(8,128)(2,1)} %w_ref.1, f32[1,3072]{1,0:T(1,128)} %bitcast.1), custom_call_target="tpu_custom_call" | custom-call | tf_op jit(solution)/shard_map/pallas_call | solution.py:407
  133.4 0.0 copy-start
  133.4 2.7 %copy.8 = bf16[256,3072]{1,0:T(8,128)(2,1)} copy(bf16[256,3072]{1,0:T(8,128)(2,1)} %get-tuple-element.4) | data formatting | bytes 3145728
  136.1 0.0 copy-done
  136.1 0.7 copy.9
Async XLA Ops:
  133.4 2.7 %copy-start = (f32[192,384]{1,0:T(8,128)S(1)}, f32[192,384]{1,0:T(8,128)}, u32[]{:S(2)}) copy-start(f32[192,384]{1,0:T(8,128)} %get-tuple-element.5) | copy-start | bytes 884740

commit v2 on v1

v2 whole, which is shorter than its diff:
```python
import functools
import math

import jax
import jax.numpy as jnp
from jax import lax
from jax.experimental import pallas as pl
from jax.experimental.pallas import tpu as pltpu
from jax.sharding import PartitionSpec as P

BLOCK = 128
EPSILON = 1e-06
SIDE = 4
TOK = 256
SHARD = 192
TILE = 768
QUARTER = 48
HALF = 384
FEATURES = 3072
MESH = pl.DeviceIdType.MESH


def hadamard_signs():
    row = lax.broadcasted_iota(jnp.int32, (BLOCK, BLOCK), 0)
    col = lax.broadcasted_iota(jnp.int32, (BLOCK, BLOCK), 1)
    common = jnp.bitwise_and(row, col)
    parity = jnp.zeros((BLOCK, BLOCK), jnp.int32)
    for shift in range(BLOCK.bit_length() - 1):
        parity = parity + jnp.bitwise_and(jnp.right_shift(common, shift), 1)
    signed = 1 - 2 * jnp.bitwise_and(parity, 1)
    return signed.astype(jnp.float32).astype(jnp.bfloat16)


def rotate(value, had):
    high = value.astype(jnp.bfloat16)
    rest = value - high.astype(jnp.float32)
    middle = rest.astype(jnp.bfloat16)
    low = (rest - middle.astype(jnp.float32)).astype(jnp.bfloat16)
    total = jnp.dot(low, had, preferred_element_type=jnp.float32)
    total = total + jnp.dot(middle, had, preferred_element_type=jnp.float32)
    total = total + jnp.dot(high, had, preferred_element_type=jnp.float32)
    return total * (1.0 / math.sqrt(BLOCK))


def kernel(
    a_ref, g_ref, w_ref, sign_ref, ig_ref, wg_ref,
    attn, grad, wq, others, staged, turned_ig, ig_v, acc, had_ref, eye, maxima, leaving, sib_in, summed, pieces, peaks, scale,
    scale_t, local_sem, a_s, a_r, g_s, g_r, w_s, w_r, h_s, h_r, o_s, o_r, i_s, i_r, m_s, m_r, q_s, q_r, p_s, p_r, c_s, c_r,
):
    dp, fsdp = lax.axis_index("dp"), lax.axis_index("fsdp")
    y, c = dp // 2, lax.rem(dp, 2)
    z, x = fsdp // SIDE, lax.rem(fsdp, SIDE)
    s = 1 - 2 * c
    off = [0, -s, s, 2]

    def mod(v):
        return lax.rem(v + 2 * SIDE, SIDE)

    def device(dx=0, dy=0, dz=0, dc=0):
        return (2 * mod(y + dy) + lax.rem(c + dc, 2), SIDE * mod(z + dz) + mod(x + dx))

    def remote(src, dst, send, recv, target):
        copy = pltpu.make_async_remote_copy(
            src_ref=src, dst_ref=dst, send_sem=send, recv_sem=recv, device_id=target, device_id_type=MESH
        )
        return copy

    sent = []

    def push(*args):
        copy = remote(*args)
        copy.start()
        sent.append(copy)
        return copy

    barrier = pltpu.get_barrier_semaphore()
    greeted = [device(dx=d) for d in range(1, SIDE)] + [device(dz=d) for d in range(1, SIDE)]
    greeted += [(lax.rem(dp + d, 8), fsdp) for d in range(1, 8)]
    for target in greeted:
        pl.semaphore_signal(barrier, inc=1, device_id=target, device_id_type=MESH)
    diagonal = x == y
    for k in range(SIDE):

        @pl.when(jnp.logical_not(jnp.logical_and(diagonal, k == y)))
        def _():
            pl.semaphore_signal(barrier, inc=1, device_id=(2 * k + c, SIDE * z + y), device_id_type=MESH)

    pl.semaphore_wait(barrier, len(greeted) + SIDE - diagonal.astype(jnp.int32))

    depth = FEATURES // 2
    k_half = pl.ds(pl.multiple_of(depth * c, depth), depth)
    y_rows = pl.ds(pl.multiple_of(QUARTER * y, QUARTER), QUARTER)

    def w_chunk(pa, pb):
        on_z = lax.select(c == 1, mod(z + off[pa]), mod(z + off[pb]))
        on_x = lax.select(c == 1, mod(x + off[pb]), mod(x + off[pa]))
        return wq.at[pl.ds(pl.multiple_of(QUARTER * (SIDE * on_z + on_x), QUARTER), QUARTER), k_half]

    def along_a(d):
        return device(dx=lax.select(c == 1, 0, d), dz=lax.select(c == 1, d, 0))

    def along_b(d):
        return device(dx=lax.select(c == 1, d, 0), dz=lax.select(c == 1, 0, d))

    w_copies = {}

    def w_push(src, dst, landing, target):
        index = 4 * landing[1] + landing[0]
        w_copies[landing] = push(src, dst, w_s.at[index], w_r.at[index], target)

    w_own = w_ref.at[y_rows, k_half]
    w_push(w_own, w_chunk(0, 0), (1, 0), along_a(s))
    w_push(w_own, w_chunk(0, 0), (2, 0), along_a(-s))
    w_push(w_own, w_chunk(0, 0), (3, 0), along_a(2))
    w_push(w_own, w_chunk(0, 0), (0, 1), along_b(s))
    w_push(w_own, w_chunk(0, 0), (0, 2), along_b(-s))
    w_push(w_own, w_chunk(0, 0), (0, 3), along_b(2))

    o_copies = [
        None,
        push(g_ref, others.at[1], o_s.at[0], o_r.at[0], device(dy=s)),
        push(g_ref, others.at[2], o_s.at[1], o_r.at[1], device(dy=-s)),
    ]

    def a_block(jx, kz):
        return attn.at[jx, pl.ds(TOK * kz, TOK)]

    def g_block(jx, kz):
        return grad.at[jx, pl.ds(TOK * kz, TOK)]

    def a_columns(owner):
        return a_ref.at[:, pl.ds(pl.multiple_of(TILE * owner, TILE), TILE)]

    def g_columns(owner):
        return g_ref.at[:, pl.ds(pl.multiple_of(TILE * owner, TILE), TILE)]

    a_copies, g_copies = {}, {}

    def a_push(src, landing, target):
        index = 4 * landing[0] + landing[1]
        a_copies[landing] = push(src, a_block(*landing), a_s.at[index], a_r.at[index], target)

    def g_push(src, landing, target):
        index = 4 * landing[0] + landing[1]
        g_copies[landing] = push(src, g_block(*landing), g_s.at[index], g_r.at[index], target)

    local = [
        pltpu.make_async_copy(a_columns(z), a_block(0, 0), local_sem.at[0]),
        pltpu.make_async_copy(g_columns(x), g_block(0, 0), local_sem.at[1]),
        pltpu.make_async_copy(g_ref, others.at[0], local_sem.at[2]),
        pltpu.make_async_copy(
            w_ref.at[y_rows, :],
            wq.at[pl.ds(pl.multiple_of(QUARTER * fsdp, QUARTER), QUARTER), :],
            local_sem.at[3],
        ),
    ]
    for copy in local:
        copy.start()
    for position, d in ((1, s), (2, -s), (3, 2)):
        a_push(a_columns(mod(z + d)), (0, position), device(dz=d))
        g_push(g_columns(mod(x + d)), (position, 0), device(dx=d))

    def a_spread(kz):
        a_push(a_block(0, kz), (1, kz), device(dx=s))
        a_push(a_block(0, kz), (2, kz), device(dx=-s))

    def g_spread(jx):
        g_push(g_block(jx, 0), (jx, 1), device(dz=s))
        g_push(g_block(jx, 0), (jx, 2), device(dz=-s))

    had_ref[...] = hadamard_signs()
    row = lax.broadcasted_iota(jnp.int32, (TOK, TOK), 0)
    col = lax.broadcasted_iota(jnp.int32, (TOK, TOK), 1)
    eye[...] = jnp.where(row == col, 1.0, 0.0).astype(eye.dtype)

    def own_blocks():
        local[0].wait()
        a_spread(0)
        local[1].wait()
        g_spread(0)

    def blocks(position):
        a_copies[0, position].wait_recv()
        a_spread(position)
        g_copies[position, 0].wait_recv()
        g_spread(position)

    shares = []

    def weight(pa, pb):
        w_copies[pa, pb].wait_recv()
        chunk = w_chunk(pa, pb)
        index = 4 * pb + pa
        shares.append(push(chunk, chunk, h_s.at[index], h_r.at[index], device(dc=1)))
        if pb == 0:
            w_push(chunk, chunk, (pa, 1), along_b(s))
            w_push(chunk, chunk, (pa, 2), along_b(-s))
            w_push(chunk, chunk, (pa, 3), along_b(2))

    def shared():
        local[2].wait()
        local[3].wait()
        for copy in shares:
            copy.wait_recv()

    def forward(i):
        a_copies[1, i].wait_recv()
        a_push(a_block(1, i), (3, i), device(dx=s))
        g_copies[i, 1].wait_recv()
        g_push(g_block(i, 1), (i, 3), device(dz=s))

    def pass_on():
        o_copies[1].wait_recv()
        o_copies.append(push(others.at[1], others.at[3], o_s.at[2], o_r.at[2], device(dy=s)))

    def partial_step(jx, low, high, first=False):
        def tile(m, carry):
            rows = pl.ds(pl.multiple_of(256 * m, 256), 256)
            value = lax.dot_general(
                attn[jx, TOK * low : TOK * high, rows],
                grad[jx, TOK * low : TOK * high, :],
                (((0,), (0,)), ((), ())),
                preferred_element_type=jnp.float32,
            )
            if first:
                acc[rows, :] = value
            else:
                acc[rows, :] += value
            return carry

        lax.fori_loop(0, TILE // 256, tile, 0)

    i_copies = []

    def slab(slot):
        if slot > 1:
            o_copies[slot].wait_recv()

        def tile(n, carry):
            rows = pl.ds(pl.multiple_of(HALF * n, HALF), HALF)
            shards = pl.ds(8 * n, 8)
            value = lax.dot_general(
                wq[rows, :], others[slot], (((1,), (1,)), ((), ())), preferred_element_type=jnp.float32
            )
            value = value.astype(staged.dtype).reshape(8, QUARTER, TOK)
            if slot == 0:
                turned_ig[shards, y_rows, :] = value
            else:
                staged[slot - 1, shards] = value
            return carry

        lax.fori_loop(0, TILE // HALF, tile, 0)
        if slot:
            landing = turned_ig.at[:, y_rows, :]
            i_copies.append(
                push(staged.at[slot - 1], landing, i_s.at[slot - 1], i_r.at[slot - 1], device(dy=off[slot]))
            )

    def write_input_grad():
        for copy in i_copies:
            copy.wait_recv()

        def tile(n, carry):
            value = lax.dot_general(
                eye[...],
                turned_ig[pl.ds(2 * n, 2)].reshape(HALF, TOK),
                (((1,), (1,)), ((), ())),
                preferred_element_type=jnp.float32,
            )
            ig_v[:, pl.ds(pl.multiple_of(HALF * n, HALF), HALF)] = value.astype(ig_v.dtype)
            return carry

        lax.fori_loop(0, FEATURES // HALF, tile, 0)
        ig_out.start()

    ig_out = pltpu.make_async_copy(ig_v, ig_ref, local_sem.at[4])

    weight(1, 0)
    weight(2, 0)
    weight(3, 0)
    own_blocks()
    weight(0, 1)
    weight(0, 2)
    weight(1, 1)
    weight(1, 2)
    weight(2, 1)
    weight(2, 2)
    weight(0, 3)
    weight(3, 1)
    weight(3, 2)
    weight(1, 3)
    weight(2, 3)
    weight(3, 3)
    blocks(1)
    blocks(2)
    blocks(3)
    pass_on()
    shared()
    slab(0)
    slab(1)
    slab(2)
    forward(0)
    forward(1)
    slab(3)
    forward(2)
    forward(3)
    partial_step(0, 0, 2, first=True)
    partial_step(1, 0, 2)

    for i in range(SIDE):
        a_copies[2, i].wait_recv()
        g_copies[i, 2].wait_recv()
    partial_step(0, 2, 3)
    partial_step(1, 2, 3)
    partial_step(2, 0, 3)
    for i in range(SIDE):
        a_copies[3, i].wait_recv()
        g_copies[i, 3].wait_recv()
        if i < 3:
            partial_step(i, 3, 4)
        partial_step(3, i, i + 1)

    maxima[...] = jnp.zeros_like(maxima)

    def turn(step, carry):
        b, m = step // 3, lax.rem(step, 3)
        rows = pl.ds(pl.multiple_of(256 * m, 256), 256)
        columns = pl.ds(pl.multiple_of(BLOCK * b, BLOCK), BLOCK)
        signs = sign_ref[:, pl.ds(pl.multiple_of(TILE * x + BLOCK * b, BLOCK), BLOCK)].astype(jnp.float32)
        turned = rotate(acc[rows, columns] * signs, had_ref[...])
        acc[rows, columns] = turned
        peak = jnp.max(jnp.abs(turned), axis=1, keepdims=True)
        lane = lax.broadcasted_iota(jnp.int32, (256, BLOCK), 1)
        maxima[rows, :] = jnp.where(lane == b, peak, maxima[rows, :])
        return carry

    lax.fori_loop(0, 18, turn, 0)
    for r in range(TILE // BLOCK):
        span = slice(BLOCK * r, BLOCK * r + BLOCK)
        peaks[0, :, span] = jnp.transpose(maxima[span, :])[:8]
    met = [
        push(peaks.at[0], peaks.at[d], m_s.at[d], m_r.at[d], (lax.rem(dp + d, 8), fsdp)) for d in range(1, 8)
    ]
    write_input_grad()
    for copy in met:
        copy.wait_recv()
    top = peaks[0]
    for d in range(1, 8):
        top = jnp.maximum(top, peaks[d])
    scale[0] = top + EPSILON

    for d in range(1, SIDE):

        @pl.when(diagonal)
        def _():
            remote(scale.at[0], scale.at[1], c_s.at[d], c_r.at[0], device(dx=d)).start()

    for r in range(TILE // BLOCK):
        span = slice(BLOCK * r, BLOCK * r + BLOCK)
        scale_t[span, :] = jnp.transpose(
            jnp.concatenate([127.0 / scale[0, :, span], jnp.ones((BLOCK - 8, BLOCK), jnp.float32)], axis=0)
        )

    def quantize(target, side, k):
        rows = slice(SHARD * k, SHARD * k + SHARD)
        for j in range(HALF // BLOCK):
            source = pl.ds(pl.multiple_of(HALF * side + BLOCK * j, BLOCK), BLOCK)
            factor = jnp.where(side == 0, scale_t[rows, j : j + 1], scale_t[rows, 3 + j : 4 + j])
            target[rows, BLOCK * j : BLOCK * j + BLOCK] = jnp.floor(acc[rows, source] * factor + 0.5).astype(target.dtype)

    traded = []
    for k in range(SIDE):
        quantize(leaving, 1 - c, k)
        span = pl.ds(SHARD * k, SHARD)
        traded.append(push(leaving.at[span, :], sib_in.at[span, :], q_s.at[k], q_r.at[k], device(dc=1)))

    def piece_copies(k):
        src = summed.at[pl.ds(SHARD * k, SHARD), :]
        here = pltpu.make_async_copy(src, pieces.at[y], p_s.at[k])
        away = remote(src, pieces.at[y], p_s.at[k], p_r.at[y], (2 * x + c, SIDE * z + k))
        return jnp.logical_and(diagonal, k == x), here, away

    for k in range(SIDE):
        quantize(summed, c, k)
        traded[k].wait_recv()
        span = slice(SHARD * k, SHARD * k + SHARD)
        summed[span, :] += sib_in[span, :]
        stays, here, away = piece_copies(k)
        pl.when(stays)(here.start)
        pl.when(jnp.logical_not(stays))(away.start)

    @pl.when(jnp.logical_not(diagonal))
    def _():
        remote(scale.at[0], scale.at[1], c_s.at[0], c_r.at[0], device(dx=1)).wait_recv()

    @pl.when(diagonal)
    def _():
        scale[1] = scale[0]
        for d in range(1, SIDE):
            remote(scale.at[0], scale.at[1], c_s.at[d], c_r.at[0], device(dx=d)).wait_send()

    for r in range(TILE // BLOCK):
        span = slice(BLOCK * r, BLOCK * r + BLOCK)
        scale_t[span, :] = jnp.transpose(
            jnp.concatenate([scale[1, :, span] / 127.0, jnp.ones((BLOCK - 8, BLOCK), jnp.float32)], axis=0)
        )
    for k in range(SIDE):
        stays, here, away = piece_copies(k)
        pl.when(stays)(here.wait)
        pl.when(jnp.logical_not(stays))(away.wait_send)
    for k in range(SIDE):
        arrives = remote(pieces.at[k], pieces.at[k], p_s.at[k], p_r.at[k], device(dx=1))
        pl.when(jnp.logical_not(jnp.logical_and(diagonal, k == y)))(arrives.wait_recv)

    rows = pl.ds(pl.multiple_of(SHARD * x, SHARD), SHARD)
    factors = scale_t[rows, :]
    for j in range(HALF // BLOCK):
        columns = slice(BLOCK * j, BLOCK * j + BLOCK)
        total = pieces[0, :, columns].astype(jnp.float32)
        for k in range(1, SIDE):
            total = total + pieces[k, :, columns].astype(jnp.float32)
        factor = jnp.where(c == 0, factors[:, j : j + 1], factors[:, 3 + j : 4 + j])
        signs = sign_ref[:, pl.ds(pl.multiple_of(HALF * dp + BLOCK * j, BLOCK), BLOCK)].astype(jnp.float32)
        wg_ref[:, columns] = rotate(total * factor, had_ref[...]) * signs

    ig_out.wait()
    for copy in sent:
        copy.wait_send()


def body(attn_out, out_grad, weight, sign_vector):
    signs = sign_vector[None, :]
    hbm = pl.BlockSpec(memory_space=pl.ANY)
    vmem = pl.BlockSpec(memory_space=pltpu.VMEM)
    dma = pltpu.SemaphoreType.DMA
    return pl.pallas_call(
        kernel,
        out_shape=(
            jax.ShapeDtypeStruct((TOK, FEATURES), jnp.bfloat16),
            jax.ShapeDtypeStruct((SHARD, HALF), jnp.float32),
        ),
        in_specs=[hbm, hbm, hbm, vmem],
        out_specs=(hbm, vmem),
        scratch_shapes=[
            pltpu.VMEM((SIDE, SIDE * TOK, TILE), jnp.bfloat16),
            pltpu.VMEM((SIDE, SIDE * TOK, TILE), jnp.bfloat16),
            pltpu.VMEM((TILE, FEATURES), jnp.bfloat16),
            pltpu.VMEM((SIDE, TOK, FEATURES), jnp.bfloat16),
            pltpu.VMEM((3, 16, QUARTER, TOK), jnp.bfloat16),
            pltpu.VMEM((16, SHARD, TOK), jnp.bfloat16),
            pltpu.VMEM((TOK, FEATURES), jnp.bfloat16),
            pltpu.VMEM((TILE, TILE), jnp.float32),
            pltpu.VMEM((BLOCK, BLOCK), jnp.bfloat16),
            pltpu.VMEM((TOK, TOK), jnp.bfloat16),
            pltpu.VMEM((TILE, BLOCK), jnp.float32),
            pltpu.VMEM((TILE, HALF), jnp.bfloat16),
            pltpu.VMEM((TILE, HALF), jnp.bfloat16),
            pltpu.VMEM((TILE, HALF), jnp.bfloat16),
            pltpu.VMEM((SIDE, SHARD, HALF), jnp.bfloat16),
            pltpu.VMEM((8, 8, TILE), jnp.float32),
            pltpu.VMEM((2, 8, TILE), jnp.float32),
            pltpu.VMEM((TILE, BLOCK), jnp.float32),
            dma((5,)), dma((16,)), dma((16,)), dma((16,)), dma((16,)), dma((16,)), dma((16,)), dma((16,)), dma((16,)),
            dma((3,)), dma((3,)), dma((3,)), dma((3,)), dma((8,)), dma((8,)), dma((4,)), dma((4,)), dma((4,)), dma((4,)),
            dma((4,)), dma((1,)),
        ],
        compiler_params=pltpu.CompilerParams(
            collective_id=0, has_side_effects=True, vmem_limit_bytes=60 * 2**20
        ),
    )(attn_out, out_grad, weight, signs)


def solution(mesh):
    in_specs = (P(("dp", "fsdp"), None), P(("dp", "fsdp"), None), P("fsdp", None), P())
    out_specs = (P(("dp", "fsdp"), None), P("fsdp", "dp"))
    return jax.shard_map(body, mesh=mesh, in_specs=in_specs, out_specs=out_specs, check_vma=False)
```

time: 137 us -> 125 us (0.912)
  Pallas kernels: 131 us -> 121 us
    pallas_call x1, Pallas kernels: 131 us -> 121 us  [body(): pl.pallas_call(kernel, out_shape=(jax.ShapeDtypeStruct((TOK, FEATURES), j...]
where the time goes in v2:
time: 125 us
  Pallas kernels  121 us (97%)
  local copies, waits for them, and re-layouts  3.41 us (3%)
    pallas_call x1, Pallas kernels, body(): pl.pallas_call(kernel, out_shape=(jax.ShapeDtypeStruct((TOK, FEATURES), j...  121 us
    unnamed x4, local copies, waits for them, and re-layouts  3.41 us

profile of v2, /device:TPU:4, one launch (start us, length us, event | category | flops | bytes accessed | tf_op | source)
XLA Modules:
  0.0 124.7 jit_solution(12402265137587727629)
XLA Ops:
  0.6 120.6 %shard_map.59 = (bf16[256,3072]{1,0:T(8,128)(2,1)}, f32[192,384]{1,0:T(8,128)}) custom-call(bf16[256,3072]{1,0:T(8,128)(2,1)} %a_ref.1, bf16[256,3072]{1,0:T(8,128)(2,1)} %g_ref.1, bf16[192,3072]{1,0:T(8,128)(2,1)} %w_ref.1, s32[1,3072]{1,0:T(1,128)} %bitcast.1), custom_call_target="tpu_custom_call" | custom-call | tf_op jit(solution)/shard_map/pallas_call | solution.py:436
  121.3 0.0 copy-start
  121.3 2.7 %copy.8 = bf16[256,3072]{1,0:T(8,128)(2,1)} copy(bf16[256,3072]{1,0:T(8,128)(2,1)} %get-tuple-element.4) | data formatting | bytes 3145728
  124.0 0.0 copy-done
  124.0 0.7 copy.9
Async XLA Ops:
  121.3 2.7 %copy-start = (f32[192,384]{1,0:T(8,128)S(1)}, f32[192,384]{1,0:T(8,128)}, u32[]{:S(2)}) copy-start(f32[192,384]{1,0:T(8,128)} %get-tuple-element.5) | copy-start | bytes 884740

commit v3 on v2

--- a/solution.py
+++ b/solution.py
@@ -21,13 +21,14 @@
 
 
 def hadamard_signs():
-    row = lax.broadcasted_iota(jnp.int32, (BLOCK, BLOCK), 0)
-    col = lax.broadcasted_iota(jnp.int32, (BLOCK, BLOCK), 1)
+    row = lax.broadcasted_iota(jnp.int32, (2 * BLOCK, 2 * BLOCK), 0)
+    col = lax.broadcasted_iota(jnp.int32, (2 * BLOCK, 2 * BLOCK), 1)
     common = jnp.bitwise_and(row, col)
-    parity = jnp.zeros((BLOCK, BLOCK), jnp.int32)
+    parity = jnp.zeros((2 * BLOCK, 2 * BLOCK), jnp.int32)
     for shift in range(BLOCK.bit_length() - 1):
         parity = parity + jnp.bitwise_and(jnp.right_shift(common, shift), 1)
     signed = 1 - 2 * jnp.bitwise_and(parity, 1)
+    signed = jnp.where(row // BLOCK == col // BLOCK, signed, 0)
     return signed.astype(jnp.float32).astype(jnp.bfloat16)
 
 
@@ -85,6 +86,12 @@
         def _():
             pl.semaphore_signal(barrier, inc=1, device_id=(2 * k + c, SIDE * z + y), device_id_type=MESH)
 
+    had_ref[...] = hadamard_signs()
+    row = lax.broadcasted_iota(jnp.int32, (TOK, TOK), 0)
+    col = lax.broadcasted_iota(jnp.int32, (TOK, TOK), 1)
+    eye[...] = jnp.where(row == col, 1.0, 0.0).astype(eye.dtype)
+
+    maxima[...] = jnp.zeros_like(maxima)
     pl.semaphore_wait(barrier, len(greeted) + SIDE - diagonal.astype(jnp.int32))
 
     depth = FEATURES // 2
@@ -114,7 +121,6 @@
     w_push(w_own, w_chunk(0, 0), (3, 0), along_a(2))
     w_push(w_own, w_chunk(0, 0), (0, 1), along_b(s))
     w_push(w_own, w_chunk(0, 0), (0, 2), along_b(-s))
-    w_push(w_own, w_chunk(0, 0), (0, 3), along_b(2))
 
     o_copies = [
         None,
@@ -168,11 +174,6 @@
         g_push(g_block(jx, 0), (jx, 1), device(dz=s))
         g_push(g_block(jx, 0), (jx, 2), device(dz=-s))
 
-    had_ref[...] = hadamard_signs()
-    row = lax.broadcasted_iota(jnp.int32, (TOK, TOK), 0)
-    col = lax.broadcasted_iota(jnp.int32, (TOK, TOK), 1)
-    eye[...] = jnp.where(row == col, 1.0, 0.0).astype(eye.dtype)
-
     def own_blocks():
         local[0].wait()
         a_spread(0)
@@ -195,7 +196,10 @@
         if pb == 0:
             w_push(chunk, chunk, (pa, 1), along_b(s))
             w_push(chunk, chunk, (pa, 2), along_b(-s))
-            w_push(chunk, chunk, (pa, 3), along_b(2))
+            if pa in ():
+                w_push(chunk, chunk, (pa, 3), along_b(2))
+        if pb == 1 and pa in (0, 1, 2, 3):
+            w_push(chunk, chunk, (pa, 3), along_b(s))
 
     def shared():
         local[2].wait()
@@ -278,27 +282,27 @@
     weight(1, 0)
     weight(2, 0)
     weight(3, 0)
+    weight(0, 1)
+    weight(1, 1)
+    weight(2, 1)
+    weight(3, 1)
     own_blocks()
-    weight(0, 1)
     weight(0, 2)
-    weight(1, 1)
     weight(1, 2)
-    weight(2, 1)
     weight(2, 2)
+    weight(3, 2)
+    pass_on()
     weight(0, 3)
-    weight(3, 1)
-    weight(3, 2)
     weight(1, 3)
     weight(2, 3)
     weight(3, 3)
     blocks(1)
     blocks(2)
     blocks(3)
-    pass_on()
     shared()
-    slab(0)
     slab(1)
     slab(2)
+    slab(0)
     forward(0)
     forward(1)
     slab(3)
@@ -320,28 +324,29 @@
             partial_step(i, 3, 4)
         partial_step(3, i, i + 1)
 
-    maxima[...] = jnp.zeros_like(maxima)
-
-    def turn(step, carry):
-        b, m = step // 3, lax.rem(step, 3)
-        rows = pl.ds(pl.multiple_of(256 * m, 256), 256)
-        columns = pl.ds(pl.multiple_of(BLOCK * b, BLOCK), BLOCK)
-        signs = sign_ref[:, pl.ds(pl.multiple_of(TILE * x + BLOCK * b, BLOCK), BLOCK)].astype(jnp.float32)
-        turned = rotate(acc[rows, columns] * signs, had_ref[...])
-        acc[rows, columns] = turned
-        peak = jnp.max(jnp.abs(turned), axis=1, keepdims=True)
-        lane = lax.broadcasted_iota(jnp.int32, (256, BLOCK), 1)
-        maxima[rows, :] = jnp.where(lane == b, peak, maxima[rows, :])
+
+    def turn(pair, carry):
+        columns = pl.ds(pl.multiple_of(2 * BLOCK * pair, 2 * BLOCK), 2 * BLOCK)
+        signs = sign_ref[:, pl.ds(pl.multiple_of(TILE * x + 2 * BLOCK * pair, BLOCK), 2 * BLOCK)].astype(jnp.float32)
+        for m in range(3):
+            rows = slice(256 * m, 256 * m + 256)
+            turned = rotate(acc[rows, columns] * signs, had_ref[...])
+            acc[rows, columns] = turned
+            size = jnp.abs(turned)
+            lane = lax.broadcasted_iota(jnp.int32, (256, BLOCK), 1)
+            first = jnp.max(size[:, :BLOCK], axis=1, keepdims=True)
+            second = jnp.max(size[:, BLOCK:], axis=1, keepdims=True)
+            found = jnp.where(lane == 2 * pair + 1, second, maxima[rows, :])
+            maxima[rows, :] = jnp.where(lane == 2 * pair, first, found)
         return carry
 
-    lax.fori_loop(0, 18, turn, 0)
+    lax.fori_loop(0, 3, turn, 0)
     for r in range(TILE // BLOCK):
         span = slice(BLOCK * r, BLOCK * r + BLOCK)
         peaks[0, :, span] = jnp.transpose(maxima[span, :])[:8]
     met = [
         push(peaks.at[0], peaks.at[d], m_s.at[d], m_r.at[d], (lax.rem(dp + d, 8), fsdp)) for d in range(1, 8)
     ]
-    write_input_grad()
     for copy in met:
         copy.wait_recv()
     top = peaks[0]
@@ -368,26 +373,34 @@
             factor = jnp.where(side == 0, scale_t[rows, j : j + 1], scale_t[rows, 3 + j : 4 + j])
             target[rows, BLOCK * j : BLOCK * j + BLOCK] = jnp.floor(acc[rows, source] * factor + 0.5).astype(target.dtype)
 
-    traded = []
-    for k in range(SIDE):
-        quantize(leaving, 1 - c, k)
-        span = pl.ds(SHARD * k, SHARD)
-        traded.append(push(leaving.at[span, :], sib_in.at[span, :], q_s.at[k], q_r.at[k], device(dc=1)))
-
     def piece_copies(k):
         src = summed.at[pl.ds(SHARD * k, SHARD), :]
         here = pltpu.make_async_copy(src, pieces.at[y], p_s.at[k])
         away = remote(src, pieces.at[y], p_s.at[k], p_r.at[y], (2 * x + c, SIDE * z + k))
         return jnp.logical_and(diagonal, k == x), here, away
 
-    for k in range(SIDE):
-        quantize(summed, c, k)
+    traded = []
+
+    def finish(k):
         traded[k].wait_recv()
         span = slice(SHARD * k, SHARD * k + SHARD)
         summed[span, :] += sib_in[span, :]
         stays, here, away = piece_copies(k)
         pl.when(stays)(here.start)
         pl.when(jnp.logical_not(stays))(away.start)
+
+    for k in range(SIDE):
+        quantize(leaving, 1 - c, k)
+        span = pl.ds(SHARD * k, SHARD)
+        traded.append(push(leaving.at[span, :], sib_in.at[span, :], q_s.at[k], q_r.at[k], device(dc=1)))
+        quantize(summed, c, k)
+        if k:
+            finish(k - 1)
+    finish(SIDE - 1)
+
+    write_input_grad()
+    for copy in sent:
+        copy.wait_send()
 
     @pl.when(jnp.logical_not(diagonal))
     def _():
@@ -421,11 +434,23 @@
             total = total + pieces[k, :, columns].astype(jnp.float32)
         factor = jnp.where(c == 0, factors[:, j : j + 1], factors[:, 3 + j : 4 + j])
         signs = sign_ref[:, pl.ds(pl.multiple_of(HALF * dp + BLOCK * j, BLOCK), BLOCK)].astype(jnp.float32)
-        wg_ref[:, columns] = rotate(total * factor, had_ref[...]) * signs
+        wg_ref[:, columns] = rotate(total * factor, had_ref[:BLOCK, :BLOCK]) * signs
 
     ig_out.wait()
-    for copy in sent:
-        copy.wait_send()
+
+
+def copy_kernel(ig_ref, wg_ref, ig_out, wg_out, ig_v, wg_v, sems):
+    steps = [(wg_ref, wg_v, wg_out, 0)]
+    for part in range(4):
+        rows = pl.ds(part * TOK // 4, TOK // 4)
+        steps.append((ig_ref.at[rows], ig_v.at[rows], ig_out.at[rows], 1 + part))
+    for source, held, _, index in steps:
+        pltpu.make_async_copy(source, held, sems.at[index]).start()
+    for source, held, target, index in steps:
+        pltpu.make_async_copy(source, held, sems.at[index]).wait()
+        pltpu.make_async_copy(held, target, sems.at[8 + index]).start()
+    for _, held, target, index in steps:
+        pltpu.make_async_copy(held, target, sems.at[8 + index]).wait()
 
 
 def body(attn_out, out_grad, weight, sign_vector):
@@ -433,7 +458,7 @@
     hbm = pl.BlockSpec(memory_space=pl.ANY)
     vmem = pl.BlockSpec(memory_space=pltpu.VMEM)
     dma = pltpu.SemaphoreType.DMA
-    return pl.pallas_call(
+    made = pl.pallas_call(
         kernel,
         out_shape=(
             jax.ShapeDtypeStruct((TOK, FEATURES), jnp.bfloat16),
@@ -450,7 +475,7 @@
             pltpu.VMEM((16, SHARD, TOK), jnp.bfloat16),
             pltpu.VMEM((TOK, FEATURES), jnp.bfloat16),
             pltpu.VMEM((TILE, TILE), jnp.float32),
-            pltpu.VMEM((BLOCK, BLOCK), jnp.bfloat16),
+            pltpu.VMEM((2 * BLOCK, 2 * BLOCK), jnp.bfloat16),
             pltpu.VMEM((TOK, TOK), jnp.bfloat16),
             pltpu.VMEM((TILE, BLOCK), jnp.float32),
             pltpu.VMEM((TILE, HALF), jnp.bfloat16),
@@ -468,6 +493,15 @@
             collective_id=0, has_side_effects=True, vmem_limit_bytes=60 * 2**20
         ),
     )(attn_out, out_grad, weight, signs)
+    return pl.pallas_call(
+        copy_kernel,
+        out_shape=tuple(jax.ShapeDtypeStruct(part.shape, part.dtype) for part in made),
+        in_specs=[hbm, hbm],
+        out_specs=(hbm, hbm),
+        scratch_shapes=[
+            pltpu.VMEM((TOK, FEATURES), jnp.bfloat16), pltpu.VMEM((SHARD, HALF), jnp.float32), dma((16,))
+        ],
+    )(*made)
 
 
 def solution(mesh):

time: 125 us -> 121 us (0.968)
  local copies, waits for them, and re-layouts: 3.41 us -> 0 us
    unnamed x4 -> x0, local copies, waits for them, and re-layouts: 3.41 us -> none
    pallas_call x1, Pallas kernels: 121 us -> 118 us  [body(): pl.pallas_call(kernel, out_shape=(jax.ShapeDtypeStruct((TOK, FEATURES), j...]
    pallas_call x0 -> x1, Pallas kernels: none -> 2.36 us  [body(): pl.pallas_call(copy_kernel, out_shape=tuple((jax.ShapeDtypeStruct(part.sh...]
where the time goes in v3:
time: 121 us
  Pallas kernels  120 us (99%)
    pallas_call x1, Pallas kernels, body(): pl.pallas_call(kernel, out_shape=(jax.ShapeDtypeStruct((TOK, FEATURES), j...  118 us

profile of v3, /device:TPU:4, one launch (start us, length us, event | category | flops | bytes accessed | tf_op | source)
XLA Modules:
  0.0 120.5 jit_solution(14263462635133638096)
XLA Ops:
  0.6 117.5 %shard_map.59 = (bf16[256,3072]{1,0:T(8,128)(2,1)}, f32[192,384]{1,0:T(8,128)}) custom-call(bf16[256,3072]{1,0:T(8,128)(2,1)} %a_ref.1, bf16[256,3072]{1,0:T(8,128)(2,1)} %g_ref.1, bf16[192,3072]{1,0:T(8,128)(2,1)} %w_ref.1, s32[1,3072]{1,0:T(1,128)} %bitcast.1), custom_call_target="tpu_custom_call" | custom-call | tf_op jit(solution)/shard_map/pallas_call | solution.py:461
  118.1 2.4 %shard_map.60 = (bf16[256,3072]{1,0:T(8,128)(2,1)}, f32[192,384]{1,0:T(8,128)}) custom-call(bf16[256,3072]{1,0:T(8,128)(2,1)} %get-tuple-element.4.ig_ref, f32[192,384]{1,0:T(8,128)} %get-tuple-element.5.wg_ref), custom_call_target="tpu_custom_call" | custom-call | tf_op jit(solution)/shard_map/pallas_call | solution.py:496

commit v4 on v3

--- a/solution.py
+++ b/solution.py
@@ -192,7 +192,6 @@
         w_copies[pa, pb].wait_recv()
         chunk = w_chunk(pa, pb)
         index = 4 * pb + pa
-        shares.append(push(chunk, chunk, h_s.at[index], h_r.at[index], device(dc=1)))
         if pb == 0:
             w_push(chunk, chunk, (pa, 1), along_b(s))
             w_push(chunk, chunk, (pa, 2), along_b(-s))
@@ -200,6 +199,7 @@
                 w_push(chunk, chunk, (pa, 3), along_b(2))
         if pb == 1 and pa in (0, 1, 2, 3):
             w_push(chunk, chunk, (pa, 3), along_b(s))
+        shares.append(push(chunk, chunk, h_s.at[index], h_r.at[index], device(dc=1)))
 
     def shared():
         local[2].wait()
@@ -366,33 +366,39 @@
             jnp.concatenate([127.0 / scale[0, :, span], jnp.ones((BLOCK - 8, BLOCK), jnp.float32)], axis=0)
         )
 
+    def quarter(k):
+        return mod(x + (2, 1, 3, 0)[k])
+
+    def quarter_rows(k):
+        return pl.ds(pl.multiple_of(SHARD * quarter(k), SHARD), SHARD)
+
     def quantize(target, side, k):
-        rows = slice(SHARD * k, SHARD * k + SHARD)
+        rows = quarter_rows(k)
         for j in range(HALF // BLOCK):
             source = pl.ds(pl.multiple_of(HALF * side + BLOCK * j, BLOCK), BLOCK)
             factor = jnp.where(side == 0, scale_t[rows, j : j + 1], scale_t[rows, 3 + j : 4 + j])
             target[rows, BLOCK * j : BLOCK * j + BLOCK] = jnp.floor(acc[rows, source] * factor + 0.5).astype(target.dtype)
 
     def piece_copies(k):
-        src = summed.at[pl.ds(SHARD * k, SHARD), :]
+        src = summed.at[quarter_rows(k), :]
         here = pltpu.make_async_copy(src, pieces.at[y], p_s.at[k])
-        away = remote(src, pieces.at[y], p_s.at[k], p_r.at[y], (2 * x + c, SIDE * z + k))
-        return jnp.logical_and(diagonal, k == x), here, away
+        away = remote(src, pieces.at[y], p_s.at[k], p_r.at[y], (2 * x + c, SIDE * z + quarter(k)))
+        return jnp.logical_and(diagonal, k == 3), here, away
 
     traded = []
 
     def finish(k):
         traded[k].wait_recv()
-        span = slice(SHARD * k, SHARD * k + SHARD)
-        summed[span, :] += sib_in[span, :]
+        rows = quarter_rows(k)
+        summed[rows, :] += sib_in[rows, :]
         stays, here, away = piece_copies(k)
         pl.when(stays)(here.start)
         pl.when(jnp.logical_not(stays))(away.start)
 
     for k in range(SIDE):
         quantize(leaving, 1 - c, k)
-        span = pl.ds(SHARD * k, SHARD)
-        traded.append(push(leaving.at[span, :], sib_in.at[span, :], q_s.at[k], q_r.at[k], device(dc=1)))
+        rows = quarter_rows(k)
+        traded.append(push(leaving.at[rows, :], sib_in.at[rows, :], q_s.at[k], q_r.at[k], device(dc=1)))
         quantize(summed, c, k)
         if k:
             finish(k - 1)

time: 121 us -> 120 us (level)
  the two profiles are of different devices: /device:TPU:4 before, /device:TPU:6 now
where the time goes in v4:
time: 120 us
  Pallas kernels  119 us (99%)
    pallas_call x1, Pallas kernels, body(): pl.pallas_call(kernel, out_shape=(jax.ShapeDtypeStruct((TOK, FEATURES), j...  117 us

profile of v4, /device:TPU:6, one launch (start us, length us, event | category | flops | bytes accessed | tf_op | source)
XLA Modules:
  0.0 119.7 jit_solution(655763593974420948)
XLA Ops:
  0.6 116.7 %shard_map.59 = (bf16[256,3072]{1,0:T(8,128)(2,1)}, f32[192,384]{1,0:T(8,128)}) custom-call(bf16[256,3072]{1,0:T(8,128)(2,1)} %a_ref.1, bf16[256,3072]{1,0:T(8,128)(2,1)} %g_ref.1, bf16[192,3072]{1,0:T(8,128)(2,1)} %w_ref.1, s32[1,3072]{1,0:T(1,128)} %bitcast.1), custom_call_target="tpu_custom_call" | custom-call | tf_op jit(solution)/shard_map/pallas_call | solution.py:467
  117.3 2.4 %shard_map.60 = (bf16[256,3072]{1,0:T(8,128)(2,1)}, f32[192,384]{1,0:T(8,128)}) custom-call(bf16[256,3072]{1,0:T(8,128)(2,1)} %get-tuple-element.4.ig_ref, f32[192,384]{1,0:T(8,128)} %get-tuple-element.5.wg_ref), custom_call_target="tpu_custom_call" | custom-call | tf_op jit(solution)/shard_map/pallas_call | solution.py:502

commit v5 on v4

--- a/solution.py
+++ b/solution.py
@@ -340,7 +340,8 @@
             maxima[rows, :] = jnp.where(lane == 2 * pair, first, found)
         return carry
 
-    lax.fori_loop(0, 3, turn, 0)
+    for pair in range(3):
+        turn(pair, 0)
     for r in range(TILE // BLOCK):
         span = slice(BLOCK * r, BLOCK * r + BLOCK)
         peaks[0, :, span] = jnp.transpose(maxima[span, :])[:8]

time: 120 us -> 119 us (level)
  no operation moved by 1% of the time
where the time goes in v5:
time: 119 us
  Pallas kernels  118 us (99%)
    pallas_call x1, Pallas kernels, body(): pl.pallas_call(kernel, out_shape=(jax.ShapeDtypeStruct((TOK, FEATURES), j...  116 us

profile of v5, /device:TPU:6, one launch (start us, length us, event | category | flops | bytes accessed | tf_op | source)
XLA Modules:
  0.0 119.0 jit_solution(14838964035467005357)
XLA Ops:
  0.6 116.0 %shard_map.59 = (bf16[256,3072]{1,0:T(8,128)(2,1)}, f32[192,384]{1,0:T(8,128)}) custom-call(bf16[256,3072]{1,0:T(8,128)(2,1)} %a_ref.1, bf16[256,3072]{1,0:T(8,128)(2,1)} %g_ref.1, bf16[192,3072]{1,0:T(8,128)(2,1)} %w_ref.1, s32[1,3072]{1,0:T(1,128)} %bitcast.1), custom_call_target="tpu_custom_call" | custom-call | tf_op jit(solution)/shard_map/pallas_call | solution.py:468
  116.7 2.4 %shard_map.60 = (bf16[256,3072]{1,0:T(8,128)(2,1)}, f32[192,384]{1,0:T(8,128)}) custom-call(bf16[256,3072]{1,0:T(8,128)(2,1)} %get-tuple-element.4.ig_ref, f32[192,384]{1,0:T(8,128)} %get-tuple-element.5.wg_ref), custom_call_target="tpu_custom_call" | custom-call | tf_op jit(solution)/shard_map/pallas_call | solution.py:503

commit v6 on v5

--- a/solution.py
+++ b/solution.py
@@ -219,7 +219,7 @@
 
     def partial_step(jx, low, high, first=False):
         def tile(m, carry):
-            rows = pl.ds(pl.multiple_of(256 * m, 256), 256)
+            rows = pl.ds(256 * m if isinstance(m, int) else pl.multiple_of(256 * m, 256), 256)
             value = lax.dot_general(
                 attn[jx, TOK * low : TOK * high, rows],
                 grad[jx, TOK * low : TOK * high, :],
@@ -232,7 +232,11 @@
                 acc[rows, :] += value
             return carry
 
-        lax.fori_loop(0, TILE // 256, tile, 0)
+        if (jx, low) == (3, 3):
+            for m in range(TILE // 256):
+                tile(m, 0)
+        else:
+            lax.fori_loop(0, TILE // 256, tile, 0)
 
     i_copies = []
 

time: 119 us -> 119 us (level)
  no operation moved by 1% of the time
where the time goes in v6:
time: 119 us; the launch traced here: 118 us
  Pallas kernels  118 us (99%)
    pallas_call x1, Pallas kernels, body(): pl.pallas_call(kernel, out_shape=(jax.ShapeDtypeStruct((TOK, FEATURES), j...  115 us

profile of v6, /device:TPU:6, one launch (start us, length us, event | category | flops | bytes accessed | tf_op | source)
XLA Modules:
  0.0 118.5 jit_solution(1561308977740182771)
XLA Ops:
  0.6 115.5 %shard_map.59 = (bf16[256,3072]{1,0:T(8,128)(2,1)}, f32[192,384]{1,0:T(8,128)}) custom-call(bf16[256,3072]{1,0:T(8,128)(2,1)} %a_ref.1, bf16[256,3072]{1,0:T(8,128)(2,1)} %g_ref.1, bf16[192,3072]{1,0:T(8,128)(2,1)} %w_ref.1, s32[1,3072]{1,0:T(1,128)} %bitcast.1), custom_call_target="tpu_custom_call" | custom-call | tf_op jit(solution)/shard_map/pallas_call | solution.py:472
  116.1 2.4 %shard_map.60 = (bf16[256,3072]{1,0:T(8,128)(2,1)}, f32[192,384]{1,0:T(8,128)}) custom-call(bf16[256,3072]{1,0:T(8,128)(2,1)} %get-tuple-element.4.ig_ref, f32[192,384]{1,0:T(8,128)} %get-tuple-element.5.wg_ref), custom_call_target="tpu_custom_call" | custom-call | tf_op jit(solution)/shard_map/pallas_call | solution.py:507
